TPU v7x, 32 devices: a whole 2x2x4 slice. The times are simulated.
32 devices in a mesh: seq: 8 (over z, y), head: 4 (over x, core).
Axes of the slice: x: 2, y: 2, z: 4, core: 2. Of those that a mesh axis runs over, the one named last changes fastest.
Arguments:
- inputs: float32 [2, 2048, 768], P(None, 'seq'), may hold values from -6 to 6
- seq_lengths: int32 [2], replicated, may hold values from 64 to 2048, as said below
- first_gain: float32 [768], replicated, may hold values from 0.5 to 1.5
- first_shift: float32 [768], replicated, may hold values from -3 to 3
- query_weight: float32 [768, 768], P(None, 'head'), may hold values from -0.21875 to 0.21875
- key_weight: float32 [768, 768], P(None, 'head'), may hold values from -0.21875 to 0.21875
- value_weight: float32 [768, 768], P(None, 'head'), may hold values from -0.21875 to 0.21875
- query_kernel: float32 [3, 768], P(None, 'head'), may hold values from -3 to 3
- key_kernel: float32 [3, 768], P(None, 'head'), may hold values from -3 to 3
- value_kernel: float32 [3, 768], P(None, 'head'), may hold values from -3 to 3
- output_weight: float32 [768, 768], P('head'), may hold values from -1.25 to 1.25
- output_bias: float32 [768], replicated, may hold values from -3 to 3
- second_gain: float32 [768], replicated, may hold values from 0.5 to 1.5
- second_shift: float32 [768], replicated, may hold values from -3 to 3
- inner_weight: float32 [768, 3072], P(None, 'head'), may hold values from -0.21875 to 0.21875
- hidden_layer_bias: float32 [3072], P('head'), may hold values from -3 to 3
- outer_weight: float32 [3072, 768], P('head'), may hold values from -0.109375 to 0.109375
- outer_bias: float32 [768], replicated, may hold values from -3 to 3
- cotangent: float32 [2, 2048, 768], P(None, 'seq'), may hold values from -6 to 6
Outputs:
- result: float32 [2, 2048, 768], P(None, 'seq')
- grad_inputs: float32 [2, 2048, 768], P(None, 'seq')
- grad_first_gain: float32 [768], replicated
- grad_first_shift: float32 [768], replicated
- grad_query_weight: float32 [768, 768], P(None, 'head')
- grad_key_weight: float32 [768, 768], P(None, 'head')
- grad_value_weight: float32 [768, 768], P(None, 'head')
- grad_query_kernel: float32 [3, 768], P(None, 'head')
- grad_key_kernel: float32 [3, 768], P(None, 'head')
- grad_value_kernel: float32 [3, 768], P(None, 'head')
- grad_output_weight: float32 [768, 768], P('head')
- grad_output_bias: float32 [768], replicated
- grad_second_gain: float32 [768], replicated
- grad_second_shift: float32 [768], replicated
- grad_inner_weight: float32 [768, 3072], P(None, 'head')
- grad_inner_bias: float32 [3072], P('head')
- grad_outer_weight: float32 [3072, 768], P('head')
- grad_outer_bias: float32 [768], replicated
Inputs may be any that keep to these rules, and one draw needn't show every extreme that they name: `seq_lengths`: in every draw one sequence, which one drawn from the seed, has all 2048 positions live.
All inputs are finite; a program needn't handle non-finite values.
Results may differ from a plain program's by a relative error of at most 0.0003.
Values sent between devices are 32-bit elements; how exact they have to be, the bound alone decides.
A program may use at most 512 MiB of HBM per device.

v0:
```python
import jax
import jax.numpy as jnp
from jax import lax
from jax.sharding import PartitionSpec as P

HSIZE = 64


EXACT_FLOAT_MODE = lax.Precision.HIGHEST
EPSILON = 1e-05
NEGATIVE = -1e30


def shifted(block, axis, distance):
    devices = range(lax.axis_size(axis))
    route = [(i - distance, i) for i in devices if i - distance in devices]
    return lax.ppermute(block, axis, route)


def matmul(input_operand, weight_matrix):
    return jnp.einsum("scd,df->scf", input_operand, weight_matrix, precision=EXACT_FLOAT_MODE)


def transposed(input_operand, weight_matrix):
    return jnp.einsum("scf,df->scd", input_operand, weight_matrix, precision=EXACT_FLOAT_MODE)


def outer_sum(first_rows, second_rows):
    return jnp.einsum("scd,scf->df", first_rows, second_rows, precision=EXACT_FLOAT_MODE)


def normalize(stream, norm_gain, norm_shift):
    centered = stream - jnp.mean(stream, -1, keepdims=True)
    inverse = lax.rsqrt(jnp.mean(centered * centered, -1, keepdims=True) + EPSILON)
    unit_rows = centered * inverse
    return (unit_rows * norm_gain + norm_shift, unit_rows, inverse)


def normalize_back(gradient, norm_gain, unit_rows, inverse):
    scaled = gradient * norm_gain
    middle = (
        scaled
        - jnp.mean(scaled, -1, keepdims=True)
        - unit_rows * jnp.mean(scaled * unit_rows, -1, keepdims=True)
    )
    return (inverse * middle, jnp.sum(gradient * unit_rows, (0, 1)), jnp.sum(gradient, (0, 1)))


def split_heads(flat):
    return flat.reshape(flat.shape[0], flat.shape[1], flat.shape[2] // HSIZE, HSIZE)


def allowed_pairs(query_pos, key_pos, lengths):
    return (key_pos[None, None, :] <= query_pos[None, :, None]) & (
        key_pos[None, None, :] < lengths[:, None, None]
    )


def pair_terms(queries, gradients, log_total, row_dots, query_pos, keyvals, key_pos, lengths):
    channels = queries.shape[2]
    query_heads = split_heads(queries)
    key_heads = split_heads(keyvals[:, :, :channels])
    value_heads = split_heads(keyvals[:, :, channels:])
    grad_heads = split_heads(gradients)
    scores = jnp.einsum(
        "sqhe,skhe->shqk", query_heads, key_heads, precision=EXACT_FLOAT_MODE
    ) * HSIZE ** (-0.5)
    allowed = allowed_pairs(query_pos, key_pos, lengths)[:, None]
    weight_values = jnp.exp(jnp.where(allowed, scores - log_total[..., None], NEGATIVE))
    weight_grads = jnp.einsum(
        "sqhe,skhe->shqk", grad_heads, value_heads, precision=EXACT_FLOAT_MODE
    )
    score_grads = weight_values * (weight_grads - row_dots[..., None])
    return (weight_values, score_grads, query_heads, key_heads, grad_heads)


def key_facing_term(terms, keyvals, channels):
    value_part = jnp.einsum("shqk,sqhe->skhe", terms[0], terms[4], precision=EXACT_FLOAT_MODE)
    key_part = jnp.einsum(
        "shqk,sqhe->skhe", terms[1], terms[2], precision=EXACT_FLOAT_MODE
    ) * HSIZE ** (-0.5)
    shape = (keyvals.shape[0], keyvals.shape[1], channels)
    return jnp.concatenate([key_part.reshape(shape), value_part.reshape(shape)], 2)


def query_side_term(terms):
    return jnp.einsum(
        "shqk,skhe->sqhe", terms[1], terms[3], precision=EXACT_FLOAT_MODE
    ) * HSIZE ** (-0.5)


def key_terms(queries, gradients, log_total, row_dots, query_pos, keyvals, key_pos, lengths):
    terms = pair_terms(
        queries, gradients, log_total, row_dots, query_pos, keyvals, key_pos, lengths
    )
    return key_facing_term(terms, keyvals, queries.shape[2])


def shards(
    inputs,
    seq_lengths,
    first_gain,
    first_shift,
    query_weight,
    key_weight,
    value_weight,
    query_kernel,
    key_kernel,
    value_kernel,
    output_weight,
    output_bias,
    second_gain,
    second_shift,
    inner_weight,
    hidden_layer_bias,
    outer_weight,
    outer_bias,
    cotangent,
):
    sequences, rows, model = inputs.shape
    channels = query_weight.shape[1]
    heads = channels // HSIZE
    positions = lax.axis_index("seq") * rows + jnp.arange(rows, dtype=jnp.int32)
    live_rows = (positions[None, :] < seq_lengths[:, None]).astype(jnp.float32)
    joined_weight = jnp.concatenate([query_weight, key_weight, value_weight], 1)
    joined_kernel = jnp.concatenate([query_kernel, key_kernel, value_kernel], 1)
    normed, leading_unit_value, first_inverse = normalize(inputs, first_gain, first_shift)
    projected = matmul(normed, joined_weight)
    rims = shifted(projected[:, rows - 2 :, :], "seq", 1)
    extended = jnp.concatenate([rims, projected], 1)
    convolved = (
        joined_kernel[0] * extended[:, 2:]
        + joined_kernel[1] * extended[:, 1:-1]
        + joined_kernel[2] * extended[:, :-2]
    )
    queries = convolved[:, :, :channels]
    keyvals = convolved[:, :, channels:]
    query_heads = split_heads(queries)
    portion = lax.all_gather(keyvals, "seq", axis=1, tiled=True)
    highest = jnp.full((sequences, heads, rows), NEGATIVE, jnp.float32)
    key_pos = jnp.arange(portion.shape[1], dtype=jnp.int32)
    key_heads = split_heads(portion[:, :, :channels])
    value_heads = split_heads(portion[:, :, channels:])
    scores = jnp.einsum(
        "sqhe,skhe->shqk", query_heads, key_heads, precision=EXACT_FLOAT_MODE
    ) * HSIZE ** (-0.5)
    allowed = allowed_pairs(positions, key_pos, seq_lengths)[:, None]
    masked = jnp.where(allowed, scores, NEGATIVE)
    new_high = jnp.maximum(highest, jnp.max(masked, -1))
    weight_values = jnp.where(allowed, jnp.exp(masked - new_high[..., None]), 0.0)
    summed = jnp.sum(weight_values, -1)
    weighted = jnp.einsum("shqk,skhe->shqe", weight_values, value_heads, precision=EXACT_FLOAT_MODE)
    highest, summed, weighted = (new_high, summed, weighted)
    log_total = highest + jnp.log(summed)
    attended = (weighted / summed[..., None]).transpose(0, 2, 1, 3).reshape(
        sequences, rows, channels
    ) * live_rows[..., None]
    branch = lax.psum(matmul(attended, output_weight), "head")
    mixed = inputs + branch + output_bias
    normed_two, second_unit, second_inverse = normalize(mixed, second_gain, second_shift)
    hidden = matmul(normed_two, inner_weight) + hidden_layer_bias
    rectified = jnp.maximum(hidden, 0.0)
    active = rectified * rectified
    result = mixed + lax.psum(matmul(active, outer_weight), "head") + outer_bias
    grad_outer_weight = outer_sum(active, cotangent)
    grad_outer_bias = jnp.sum(cotangent, (0, 1))
    grad_hidden = transposed(cotangent, outer_weight) * (2.0 * rectified)
    grad_inner_weight = outer_sum(normed_two, grad_hidden)
    grad_inner_bias = jnp.sum(grad_hidden, (0, 1))
    grad_normed_two = lax.psum(transposed(grad_hidden, inner_weight), "head")
    through_two, grad_second_gain, grad_second_shift = normalize_back(
        grad_normed_two, second_gain, second_unit, second_inverse
    )
    grad_mixed = cotangent + through_two
    grad_output_weight = outer_sum(attended, grad_mixed)
    grad_output_bias = jnp.sum(grad_mixed, (0, 1))
    grad_attended = transposed(grad_mixed, output_weight) * live_rows[..., None]
    row_dots = jnp.sum(split_heads(grad_attended) * split_heads(attended), -1).transpose(0, 2, 1)
    portion = lax.all_gather(keyvals, "seq", axis=1, tiled=True)
    key_pos = jnp.arange(portion.shape[1], dtype=jnp.int32)
    terms = pair_terms(
        queries, grad_attended, log_total, row_dots, positions, portion, key_pos, seq_lengths
    )
    grad_queries = query_side_term(terms).reshape(jnp.zeros_like(queries).shape)
    query_side = jnp.concatenate([queries, grad_attended], 2)
    row_stats = jnp.concatenate([log_total, row_dots], 1).transpose(0, 2, 1)
    side_rows = lax.all_gather(query_side, "seq", axis=1, tiled=True)
    stat_rows = lax.all_gather(row_stats, "seq", axis=1, tiled=True)
    query_pos = jnp.arange(side_rows.shape[1], dtype=jnp.int32)
    portion_total = stat_rows[:, :, :heads].transpose(0, 2, 1)
    portion_dots = stat_rows[:, :, heads:].transpose(0, 2, 1)
    grad_keyvals = key_terms(
        side_rows[:, :, :channels],
        side_rows[:, :, channels:],
        portion_total,
        portion_dots,
        query_pos,
        keyvals,
        positions,
        seq_lengths,
    )
    grad_convolved = jnp.concatenate([grad_queries, grad_keyvals], 2)
    following = shifted(grad_convolved[:, :2, :], "seq", -1)
    grad_extended = jnp.concatenate([grad_convolved, following], 1)
    grad_projected = (
        joined_kernel[0] * grad_extended[:, :rows]
        + joined_kernel[1] * grad_extended[:, 1 : rows + 1]
        + joined_kernel[2] * grad_extended[:, 2:]
    )
    grad_kernel = jnp.stack(
        [
            jnp.sum(grad_convolved * extended[:, 2:], (0, 1)),
            jnp.sum(grad_convolved * extended[:, 1:-1], (0, 1)),
            jnp.sum(grad_convolved * extended[:, :-2], (0, 1)),
        ]
    )
    grad_joined = outer_sum(normed, grad_projected)
    grad_normed = lax.psum(transposed(grad_projected, joined_weight), "head")
    through_one, grad_first_gain, grad_first_shift = normalize_back(
        grad_normed, first_gain, leading_unit_value, first_inverse
    )
    grad_inputs = grad_mixed + through_one
    grad_query_weight = grad_joined[:, :channels]
    grad_key_weight = grad_joined[:, channels : 2 * channels]
    grad_value_weight = grad_joined[:, 2 * channels :]
    grad_query_kernel = grad_kernel[:, :channels]
    grad_key_kernel = grad_kernel[:, channels : 2 * channels]
    grad_value_kernel = grad_kernel[:, 2 * channels :]
    (
        grad_first_gain,
        grad_first_shift,
        grad_query_weight,
        grad_key_weight,
        grad_value_weight,
        grad_query_kernel,
        grad_key_kernel,
        grad_value_kernel,
        grad_output_weight,
        grad_output_bias,
        grad_second_gain,
        grad_second_shift,
        grad_inner_weight,
        grad_inner_bias,
        grad_outer_weight,
        grad_outer_bias,
    ) = lax.psum(
        (
            grad_first_gain,
            grad_first_shift,
            grad_query_weight,
            grad_key_weight,
            grad_value_weight,
            grad_query_kernel,
            grad_key_kernel,
            grad_value_kernel,
            grad_output_weight,
            grad_output_bias,
            grad_second_gain,
            grad_second_shift,
            grad_inner_weight,
            grad_inner_bias,
            grad_outer_weight,
            grad_outer_bias,
        ),
        "seq",
    )
    return (
        result,
        grad_inputs,
        grad_first_gain,
        grad_first_shift,
        grad_query_weight,
        grad_key_weight,
        grad_value_weight,
        grad_query_kernel,
        grad_key_kernel,
        grad_value_kernel,
        grad_output_weight,
        grad_output_bias,
        grad_second_gain,
        grad_second_shift,
        grad_inner_weight,
        grad_inner_bias,
        grad_outer_weight,
        grad_outer_bias,
    )


def solution(mesh):
    return jax.shard_map(
        shards,
        mesh=mesh,
        in_specs=(
            P(None, "seq", None),
            P(),
            P(),
            P(),
            P(None, "head"),
            P(None, "head"),
            P(None, "head"),
            P(None, "head"),
            P(None, "head"),
            P(None, "head"),
            P("head", None),
            P(),
            P(),
            P(),
            P(None, "head"),
            P("head"),
            P("head", None),
            P(),
            P(None, "seq", None),
        ),
        out_specs=(
            P(None, "seq", None),
            P(None, "seq", None),
            P(),
            P(),
            P(None, "head"),
            P(None, "head"),
            P(None, "head"),
            P(None, "head"),
            P(None, "head"),
            P(None, "head"),
            P("head", None),
            P(),
            P(),
            P(),
            P(None, "head"),
            P("head"),
            P("head", None),
            P(),
        ),
        check_vma=False,
    )
```

profile of v0, /device:TPU:0, one launch (start us, length us, event | category | flops | bytes accessed | tf_op | source)
XLA Modules:
  0.0 798.7 jit_solution(10545995388507133922)
XLA Ops:
  7.3 1.7 reduce_sum.180
  9.0 1.8 multiply_reduce_fusion.5
  10.9 4.7 fusion.46
  16.8 1.9 copy.39
  18.7 5.5 collective-permute-start
  25.1 1.8 copy.40
  26.9 2.3 multiply_add_fusion.8
  35.2 98.2 %all-gather.3.cloned.1.call-done = f32[2,2048,384]{1,2,0:T(8,128)} async-done(((f32[2,256,384]{1,2,0:T(8,128)}), f32[2,2048,384]{1,2,0:T(8,128)}) %all-gather.3.cloned.1.call-update) | async-done | bytes 6291472 | tf_op jit(solution)/shard_map/all_gather | solution.py:139
  133.5 5.2 fusion.94
  138.7 12.6 %select_reduce_fusion = (f32[2,3,256]{2,1,0:T(4,128)S(1)}, f32[2,3,256,2048]{3,2,1,0:T(8,128)S(1)}) fusion(pred[2,256,2048]{2,1,0:T(8,128)(4,1)S(1)} %broadcast_and_fusion.1, f32[2,256,3,64]{1,3,2,0:T(8,128)S(1)} %bitcast.105, f32[2,2048,3,64]{1,3,2,0:T(8,128)S(1)} %bitcast.86), kind=kOutput, calls=%fused_computation.11 | convolution fusion | flops 2425354752 | bytes 17176576 | tf_op jit(solution)/shard_map/sqhe,skhe->shqk/dot_general | solution.py:144
  151.3 4.1 fusion.11
  155.8 17.3 %fusion.58 = f32[2,256,3,64]{1,3,2,0:T(8,128)S(1)} fusion(f32[2,2048,3,64]{1,3,2,0:T(8,128)} %bitcast.90, f32[2,3,256,2048]{3,2,1,0:T(8,128)} %copy-done.1, f32[2,3,256]{2,1,0:T(4,128)S(1)} %broadcast_maximum_fusion, pred[2,256,2048]{2,1,0:T(8,128)(4,1)S(1)} %broadcast_and_fusion.1, f32[2,256,3]{1,2,0:T(4,128)S(1)} %bitcast.110), kind=kOutput, calls=%fused_computation.92 | convolution fusion | flops 2428600320 | bytes 17182720 | tf_op jit(solution)/shard_map/shqk,skhe->shqe/dot_general | solution.py:152
  174.7 2.6 fusion.76
  177.5 41.0 %all-reduce.8.cloned.1.call-done = f32[2,256,768]{2,1,0:T(8,128)} async-done(((f32[2,256,768]{2,1,0:T(8,128)}), f32[2,256,768]{2,1,0:T(8,128)}) %all-reduce.8.cloned.1.call-update) | async-done | bytes 1572880 | tf_op jit(solution)/shard_map/psum | solution.py:158
  218.5 2.3 fusion.91
  221.7 4.2 add_maximum_fusion
  226.0 4.7 fusion.98
  231.9 5.4 fusion.36
  237.3 43.0 %all-reduce.10.cloned.1.call-done = f32[2,256,768]{2,1,0:T(8,128)} async-done(((f32[2,256,768]{2,1,0:T(8,128)}), f32[2,256,768]{2,1,0:T(8,128)}) %all-reduce.10.cloned.1.call-update) | async-done | bytes 1572880 | tf_op jit(solution)/shard_map/psum | solution.py:170
  280.3 3.3 multiply_reduce_fusion
  283.7 2.7 fusion.90
  287.6 1.8 convolution_multiply_fusion
  294.2 31.3 %all_gather.12 = f32[2,2048,6]{1,2,0:T(8,128)S(1)} all-gather(f32[2,256,6]{1,2,0:T(8,128)S(1)} %maximum_bitcast_fusion.3), channel_id=1, replica_groups=mesh['seq'=8,'head'=4] {'seq'}, dimensions={1}, use_global_device_ids=true | all-gather | bytes 110592 | tf_op jit(solution)/shard_map/all_gather | solution.py:188
  326.2 11.3 %fusion.99 = f32[2,3,256,2048]{3,2,1,0:T(8,128)S(1)} fusion(f32[2,256,3,64]{1,3,2,0:T(8,128)} %bitcast.101, f32[2,2048,3,64]{1,3,2,0:T(8,128)S(1)} %bitcast.91), kind=kOutput, calls=%fused_computation.157 | convolution fusion | flops 2415919104 | bytes 16121856 | tf_op jit(solution)/shard_map/sqhe,skhe->shqk/dot_general | solution.py:70
  337.4 19.1 %fusion.49 = f32[2,3,64,256]{3,2,1,0:T(8,128)} fusion(f32[2,2048,3,64]{1,3,2,0:T(8,128)} %bitcast.87, f32[2,3,256,2048]{3,2,1,0:T(8,128)S(1)} %fusion.99, f32[2,3,256,2048]{3,2,1,0:T(8,128)} %copy-done.1, f32[2,3,256]{2,1,0:T(4,128)S(1)} %bitcast.109, f32[2,3,256]{2,1,0:T(4,128)S(1)} %log_add_fusion, pred[2,256,2048]{2,1,0:T(8,128)(4,1)S(1)} %broadcast_and_fusion.1), kind=kOutput, calls=%fused_computation.79 | convolution fusion | flops 2431746048 | bytes 29765632 | tf_op jit(solution)/shard_map/shqk,skhe->sqhe/dot_general | solution.py:87
  356.6 36.7 %all-gather.5.cloned.1.call-done = f32[2,2048,384]{1,2,0:T(8,128)} async-done(((f32[2,256,384]{1,2,0:T(8,128)}), f32[2,2048,384]{1,2,0:T(8,128)}) %all-gather.5.cloned.1.call-update) | async-done | bytes 6291472 | tf_op jit(solution)/shard_map/all_gather | solution.py:187
  393.3 3.3 fusion.93
  396.6 10.0 %fusion.101 = f32[2,3,2048,256]{3,2,1,0:T(8,128)S(1)} fusion(f32[2,2048,3,64]{1,3,2,0:T(8,128)S(1)} %bitcast.92, f32[2,256,3,64]{1,3,2,0:T(8,128)S(1)} %bitcast.107), kind=kOutput, calls=%fused_computation.159 | convolution fusion | flops 2415919104 | bytes 16121856 | tf_op jit(solution)/shard_map/sqhe,skhe->shqk/dot_general | solution.py:70
  406.6 12.7 %fusion.100 = f32[2,3,2048,256]{3,2,1,0:T(8,128)} fusion(f32[2,2048,3,64]{1,3,2,0:T(8,128)S(1)} %bitcast.88, f32[2,256,3,64]{1,3,2,0:T(8,128)S(1)} %bitcast.106), kind=kOutput, calls=%fused_computation.158 | convolution fusion | flops 2415919104 | bytes 16121856 | tf_op jit(solution)/shard_map/sqhe,skhe->shqk/dot_general | solution.py:65
  419.3 12.3 %fusion.10 = f32[2,3,64,256]{3,2,1,0:T(8,128)S(1)} fusion(f32[2,2048,3,64]{1,3,2,0:T(8,128)S(1)} %bitcast.93, f32[2,3,2048,256]{3,2,1,0:T(8,128)} %fusion.100, f32[2,3,2048]{2,1,0:T(4,128)S(1)} %copy-done.49, pred[2,2048,256]{2,1,0:T(8,128)(4,1)S(1)} %copy-done.28), kind=kOutput, calls=%fused_computation.13 | convolution fusion | flops 2425356288 | bytes 17219584 | tf_op jit(solution)/shard_map/shqk,sqhe->skhe/dot_general | solution.py:78
  431.6 13.5 %fusion.52 = f32[2,3,64,256]{3,2,1,0:T(8,128)S(1)} fusion(f32[2,2048,3,64]{1,3,2,0:T(8,128)S(1)} %bitcast.89, f32[2,3,2048,256]{3,2,1,0:T(8,128)S(1)} %fusion.101, f32[2,3,2048,256]{3,2,1,0:T(8,128)} %fusion.100, f32[2,3,2048]{2,1,0:T(4,128)S(1)} %copy-done.48, f32[2,3,2048]{2,1,0:T(4,128)S(1)} %copy-done.49, pred[2,2048,256]{2,1,0:T(8,128)(4,1)S(1)} %copy-done.28), kind=kOutput, calls=%fused_computation.80 | convolution fusion | flops 2431746048 | bytes 29851648 | tf_op jit(solution)/shard_map/shqk,sqhe->skhe/dot_general | solution.py:79
  446.0 1.9 copy.41
  447.9 1.7 collective-permute-start.1
  449.6 6.6 fusion.34
  456.2 1.8 copy.42
  459.7 3.9 multiply_reduce_fusion.9
  463.6 5.2 fusion.47
  469.1 7.5 convolution_bitcast_fusion
  476.7 5.8 convolution_bitcast_fusion.1
  482.5 2.0 convolution_bitcast_fusion.3
  484.5 3.7 convolution_bitcast_fusion.2
  490.3 48.0 %all-reduce.14.cloned.1.call-done = (f32[2,256,768]{2,1,0:T(8,128)}, f32[2,256,768]{2,1,0:T(8,128)}) async-done(((f32[2,256,768]{2,1,0:T(8,128)}, f32[2,256,768]{2,1,0:T(8,128)}), (f32[2,256,768]{2,1,0:T(8,128)}, f32[2,256,768]{2,1,0:T(8,128)})) %all-reduce.14.cloned.1.call-update) | async-done | bytes 3145744 | tf_op jit(solution)/shard_map/psum | solution.py:164
  538.4 2.7 multiply_reduce_fusion.1
  541.1 40.3 %all-reduce = (f32[768]{0:T(1024)}, f32[768]{0:T(1024)}, f32[3,192]{1,0:T(4,128)}, f32[3,192]{1,0:T(4,128)}, f32[3,192]{1,0:T(4,128)}, /*index=5*/f32[768]{0:T(1...) all-reduce(f32[768]{0:T(1024)S(1)} %get-tuple-element.20, ...), channel_id=1, replica_groups=mesh['seq'=8,'head'=4] {'seq'}, use_global_device_ids=true, to_apply=%region_16.17 | all-reduce | flops 7104 | bytes 56832 | tf_op jit(solution)/shard_map/psum | solution.py:246
  581.4 3.4 add_add_fusion
  584.9 1.7 multiply_add_fusion
  586.6 196.6 %all-reduce.12.cloned.1.call-done = (f32[768,192]{0,1:T(8,128)}, f32[768,192]{0,1:T(8,128)}, f32[768,192]{0,1:T(8,128)}, f32[192,768]{1,0:T(8,128)}, f32[768,768]{1,0:T(8,128)}, /*index=5*/f32[768,768]{1,0:T(8,128)}) async-done(((f32[768,192]{0,1:T(8,128)}, f32[768,192]{0,1:T(8,128)}, f32[768,192]{0,1:T(8,128)}, f32[192,768]{1,0:T(8,128)}, f32[768,768]{1,0:T(8,128)}, /*index=5*/f32[768,768]{1,0:T(8,128)}), ...) | async-done | bytes 7077904 | tf_op jit(solution)/shard_map/psum | solution.py:246
  783.2 2.0 copy.57
  (204 shorter events, 30.6 us)
Async XLA Ops:
  7.2 218.8 %copy-start = (f32[768,768]{1,0:T(8,128)S(1)}, f32[768,768]{1,0:T(8,128)}, u32[]{:S(2)}) copy-start(f32[768,768]{1,0:T(8,128)} %param.35) | copy-start | bytes 7077892
  7.2 3.6 copy-start.54
  7.2 3.6 copy-start.71
  7.2 126.2 %all-gather.3.cloned.1.call-start = ((), (), s32[]{:S(2)}) async-start(), calls=%async_computation | async-start | bytes 7077888 | tf_op jit(solution)/shard_map/all_gather | solution.py:139
  10.9 4.7 copy-start.56
  15.6 13.6 %copy-start.20 = (f32[2,256,576]{1,2,0:T(8,128)}, f32[2,256,576]{1,2,0:T(8,128)S(1)}, u32[]{:S(2)}) copy-start(f32[2,256,576]{1,2,0:T(8,128)S(1)} %fusion.46) | copy-start | bytes 3538948
  18.7 6.4 collective-permute-start
  25.1 4.2 copy-start.50
  31.2 187.3 %all-reduce.8.cloned.1.call-start = ((), (), s32[]{:S(2)}) async-start(), calls=%async_computation.1 | async-start | bytes 3145728 | tf_op jit(solution)/shard_map/psum | solution.py:158
  133.4 5.2 copy-start.32
  138.7 12.6 %copy-start.8 = (f32[2,2048,192]{1,2,0:T(8,128)}, f32[2,2048,192]{1,2,0:T(8,128)S(1)}, u32[]{:S(2)}) copy-start(f32[2,2048,192]{1,2,0:T(8,128)S(1)} %get-tuple-element.58) | copy-start | bytes 9437188
  151.3 4.5 copy-start.1
  155.8 18.9 %copy-start.36 = (f32[192,768]{1,0:T(8,128)S(1)}, f32[192,768]{1,0:T(8,128)}, u32[]{:S(2)}) copy-start(f32[192,768]{1,0:T(8,128)} %param.29) | copy-start | bytes 1769476
  174.7 43.8 %copy-start.68 = (f32[768]{0:T(1024)S(1)}, f32[768]{0:T(1024)}, u32[]{:S(2)}) copy-start(f32[768]{0:T(1024)} %param.30) | copy-start | bytes 9220
  177.3 103.0 %all-reduce.10.cloned.1.call-start = ((), (), s32[]{:S(2)}) async-start(), calls=%async_computation.2 | async-start | bytes 3145728 | tf_op jit(solution)/shard_map/psum | solution.py:170
  220.8 5.1 copy-start.5
  221.7 62.0 %copy-start.58 = (f32[2,256]{1,0:T(2,128)}, f32[2,256]{1,0:T(2,128)S(1)}, u32[]{:S(2)}) copy-start(f32[2,256]{1,0:T(2,128)S(1)} %add_rsqrt_fusion) | copy-start | bytes 6148
  221.7 4.3 copy-start.12
  226.0 4.7 copy-start.16
  237.3 156.0 %all-gather.5.cloned.1.call-start = ((), (), s32[]{:S(2)}) async-start(), calls=%async_computation.3 | async-start | bytes 7077888 | tf_op jit(solution)/shard_map/all_gather | solution.py:187
  283.7 3.9 copy-start.37
  286.4 3.7 copy-start.33
  291.1 247.2 %all-reduce.14.cloned.1.call-start = ((), (), s32[]{:S(2)}) async-start(), calls=%async_computation.5 | async-start | bytes 6291456 | tf_op jit(solution)/shard_map/psum | solution.py:164
  291.2 35.0 %copy-start.17 = (f32[2,2048,192]{1,2,0:T(8,128)S(1)}, f32[2,2048,192]{1,2,0:T(8,128)}, u32[]{:S(2)}) copy-start(f32[2,2048,192]{1,2,0:T(8,128)} %get-tuple-element.59) | copy-start | bytes 9437188
  356.6 40.0 %copy-start.41 = (f32[2,256,192]{1,2,0:T(8,128)S(1)}, f32[2,256,192]{1,2,0:T(8,128)}, u32[]{:S(2)}) copy-start(f32[2,256,192]{1,2,0:T(8,128)} %get-tuple-element.65) | copy-start | bytes 1179652
  396.6 10.0 %copy-start.40 = (f32[2,256,192]{1,2,0:T(8,128)S(1)}, f32[2,256,192]{1,2,0:T(8,128)}, u32[]{:S(2)}) copy-start(f32[2,256,192]{1,2,0:T(8,128)} %get-tuple-element.66) | copy-start | bytes 1179652
  406.6 12.7 %copy-start.28 = (pred[2,2048,256]{2,1,0:T(8,128)(4,1)S(1)}, pred[2,2048,256]{2,1,0:T(8,128)(4,1)}, u32[]{:S(2)}) copy-start(pred[2,2048,256]{2,1,0:T(8,128)(4,1)} %broadcast_and_fusion) | copy-start | bytes 3145732
  406.6 12.7 %copy-start.49 = (f32[2,3,2048]{2,1,0:T(4,128)S(1)}, f32[2,3,2048]{2,1,0:T(4,128)}, u32[]{:S(2)}) copy-start(f32[2,3,2048]{2,1,0:T(4,128)} %get-tuple-element.69) | copy-start | bytes 147460
  419.3 12.3 %copy-start.48 = (f32[2,3,2048]{2,1,0:T(4,128)S(1)}, f32[2,3,2048]{2,1,0:T(4,128)}, u32[]{:S(2)}) copy-start(f32[2,3,2048]{2,1,0:T(4,128)} %get-tuple-element.68) | copy-start | bytes 147460
  431.6 26.4 %copy-start.29 = (f32[2,3,64,256]{3,2,1,0:T(8,128)}, f32[2,3,64,256]{3,2,1,0:T(8,128)S(1)}, u32[]{:S(2)}) copy-start(f32[2,3,64,256]{3,2,1,0:T(8,128)S(1)} %fusion.10) | copy-start | bytes 1179652
  431.6 13.5 %copy-start.22 = (f32[2,3,64,256]{3,2,1,0:T(8,128)S(1)}, f32[2,3,64,256]{3,2,1,0:T(8,128)}, u32[]{:S(2)}) copy-start(f32[2,3,64,256]{3,2,1,0:T(8,128)} %fusion.49) | copy-start | bytes 1179652
  445.1 12.9 %copy-start.24 = (f32[2,3,64,256]{3,2,1,0:T(8,128)}, f32[2,3,64,256]{3,2,1,0:T(8,128)S(1)}, u32[]{:S(2)}) copy-start(f32[2,3,64,256]{3,2,1,0:T(8,128)S(1)} %fusion.52) | copy-start | bytes 1179652
  447.9 8.3 %collective-permute-start.1 = (f32[2,2,576]{2,1,0:T(2,128)}, f32[2,2,576]{2,1,0:T(2,128)}, u32[]{:S(2)}, u32[]{:S(2)}) collective-permute-start(f32[2,2,576]{2,1,0:T(2,128)} %copy.41), channel_id=1, source_target_pairs={{4,0},{8,4},{12,8},{16,12},{20,16},{24,20},{28,24},{5,1},{9,5},{13... | collective-permute-start | bytes 27656 | tf_op jit(solution)/shard_map/ppermute | solution.py:17
  459.7 3.9 copy-start.42
  459.7 3.9 copy-start.43
  459.7 3.9 copy-start.44
  468.8 7.8 copy-start.53
  468.8 7.8 copy-start.59
  468.8 314.4 %all-reduce.12.cloned.1.call-start = ((), (), s32[]{:S(2)}) async-start(), calls=%async_computation.4 | async-start | bytes 14155776 | tf_op jit(solution)/shard_map/psum | solution.py:246
  469.0 7.6 copy-start.7
  469.1 7.6 copy-start.15
  469.1 7.6 copy-start.70
  476.6 5.8 copy-start.10
  476.6 5.8 copy-start.31
  538.4 43.0 %copy-start.73 = (f32[768]{0:T(1024)S(1)}, f32[768]{0:T(1024)}, u32[]{:S(2)}) copy-start(f32[768]{0:T(1024)} %param.36) | copy-start | bytes 9220
  581.4 3.4 copy-start.4
  581.4 3.5 copy-start.25
  783.2 3.7 copy-start.45
  (35 other events, 65.5 us)
Sparse Core Ops, SparseCore 0:
  31.4 102.0 all-gather.2
  177.4 41.0 all-reduce.7
  237.4 42.8 all-reduce.9
  291.2 101.9 all-gather.4
  468.9 69.3 all-reduce.13
  545.0 238.1 all-reduce.11
where the time goes:
time: 804 us; the launch traced here: 799 us
  waiting for transfers between devices  464 us (58%)
  matrix products  163 us (20%)
  blocking collectives  71.6 us (9%)
  other arithmetic  39 us (5%)
  local copies, waits for them, and re-layouts  38.2 us (5%)
  between operations  15.2 us (2%)
    psum x1, waiting for transfers between devices, shards(): lax.psum((grad_first_gain, grad_first_shift, grad_query_weight, grad_key_...  197 us
    all_gather x1, waiting for transfers between devices, shards(): portion = lax.all_gather(keyvals, 'seq', axis=1, tiled=True)  98.2 us
    psum x1, waiting for transfers between devices, shards(): result = mixed + lax.psum(matmul(active, outer_weight), 'head') + outer_bias  48 us
    psum x1, waiting for transfers between devices, shards(): grad_normed_two = lax.psum(transposed(grad_hidden, inner_weight), 'head')  43 us
    psum x1, waiting for transfers between devices, shards(): branch = lax.psum(matmul(attended, output_weight), 'head')  41 us
    psum x1, blocking collectives, shards(): lax.psum((grad_first_gain, grad_first_shift, grad_query_weight, grad_key_...  40.3 us
    all_gather x1, waiting for transfers between devices, shards(): side_rows = lax.all_gather(query_side, 'seq', axis=1, tiled=True)  36.7 us
    all_gather x1, blocking collectives, shards(): stat_rows = lax.all_gather(row_stats, 'seq', axis=1, tiled=True)  31.3 us
  transfers between devices with their start and end apart: 8, of which 6 were waited for; matrix products, arithmetic and copies ran while one was open for 9% of the time, Pallas kernels for 0%

commit v1 on v0

--- a/solution.py
+++ b/solution.py
@@ -1,12 +1,18 @@
+import functools
+
 import jax
 import jax.numpy as jnp
 from jax import lax
+from jax.experimental import pallas as pl
+from jax.experimental.pallas import tpu as pltpu
 from jax.sharding import PartitionSpec as P
 
+MESH = pl.DeviceIdType.MESH
+
 HSIZE = 64
 
 
-EXACT_FLOAT_MODE = lax.Precision.HIGHEST
+EXACT_FLOAT_MODE = lax.Precision.HIGH
 EPSILON = 1e-05
 NEGATIVE = -1e30
 
@@ -96,7 +102,7 @@
     return key_facing_term(terms, keyvals, queries.shape[2])
 
 
-def shards(
+def general_shards(
     inputs,
     seq_lengths,
     first_gain,
@@ -176,8 +182,6 @@
     grad_output_bias = jnp.sum(grad_mixed, (0, 1))
     grad_attended = transposed(grad_mixed, output_weight) * live_rows[..., None]
     row_dots = jnp.sum(split_heads(grad_attended) * split_heads(attended), -1).transpose(0, 2, 1)
-    portion = lax.all_gather(keyvals, "seq", axis=1, tiled=True)
-    key_pos = jnp.arange(portion.shape[1], dtype=jnp.int32)
     terms = pair_terms(
         queries, grad_attended, log_total, row_dots, positions, portion, key_pos, seq_lengths
     )
@@ -286,9 +290,1347 @@
     )
 
 
+class Comm:
+    def __init__(self, send_sems, recv_sems, local_sems=None):
+        self.send_sems, self.recv_sems, self.local_sems = send_sems, recv_sems, local_sems
+        self.used = 0
+        self.used_local = 0
+        self.sent = []
+        self.stored = []
+
+    def copy(self, source, target, device, when=None):
+        index = self.used
+        self.used += 1
+        made = pltpu.make_async_remote_copy(
+            src_ref=source,
+            dst_ref=target,
+            send_sem=self.send_sems.at[index],
+            recv_sem=self.recv_sems.at[index],
+            device_id=device,
+            device_id_type=MESH,
+        )
+        if when is None:
+            made.start()
+        else:
+            pl.when(when)(made.start)
+        self.sent.append((made, when))
+        return made
+
+    def settle(self, made):
+        self.sent = [one for one in self.sent if one[0] is not made]
+        made.wait_send()
+
+    def local(self, source, target, when=None, keep=True):
+        made = pltpu.make_async_copy(source, target, self.local_sems.at[self.used_local])
+        self.used_local += 1
+        if when is None:
+            made.start()
+        else:
+            pl.when(when)(made.start)
+        if keep:
+            self.stored.append((made, when))
+        return made
+
+    def finish(self):
+        for made, when in self.sent:
+            if when is None:
+                made.wait_send()
+            else:
+                pl.when(when)(made.wait_send)
+        for made, when in self.stored:
+            if when is None:
+                made.wait()
+            else:
+                pl.when(when)(made.wait)
+
+
+def wait_for(made, when=None):
+    if when is None:
+        made.wait_recv()
+    else:
+        pl.when(when)(made.wait_recv)
+
+
+class Place:
+    def __init__(self):
+        self.seq = lax.axis_index("seq")
+        self.head = lax.axis_index("head")
+        self.z = self.seq // 2
+        self.y = self.seq % 2
+        self.other = 1 - self.y
+        self.core = self.head % 2
+        self.at_end = (self.z == 0) | (self.z == LINE - 1)
+        self.at_middle = jnp.logical_not(self.at_end)
+        step = 2 - 4 * (self.z // 2)
+        self.pair = (2 * self.z + self.other, self.head)
+        self.inward = (self.seq + step, self.head)
+        self.outward = (self.seq - step, self.head)
+        self.sibling = (self.seq, self.head + 1 - 2 * self.core)
+        self.facing = (self.seq, (self.head + 2) % 4)
+
+
+LINE = 4
+
+
+def rows_at(ref, start, count):
+    return ref.at[pl.ds(pl.multiple_of(start, 8), count)]
+
+
+class Land:
+    def __init__(self, ref):
+        self.ref, self.used = ref, 0
+
+    def take(self, rows):
+        got = self.ref.at[pl.ds(self.used, rows)]
+        self.used += rows
+        return got
+
+
+def sum_pair_first(comm, place, land, source, target, start, count):
+    half = count // 2
+    line, from_end, from_middle = land.take(half), land.take(half), land.take(half)
+    own = rows_at(target, start + place.y * half, half)
+    far = rows_at(source, start + place.other * half, half)
+    near = rows_at(source, start + place.y * half, half)
+    made = comm.copy(far, line, place.pair)
+    yield
+    made.wait_recv()
+    line[...] = line[...] + near[...]
+    inward = comm.copy(line, from_end, place.inward, place.at_end)
+    yield
+
+    @pl.when(place.at_middle)
+    def _():
+        inward.wait_recv()
+        from_end[...] = from_end[...] + line[...]
+
+    across = comm.copy(from_end, from_middle, place.inward, place.at_middle)
+    yield
+
+    @pl.when(place.at_middle)
+    def _():
+        across.wait_recv()
+        from_middle[...] = from_middle[...] + from_end[...]
+
+    outward = comm.copy(from_middle, own, place.outward, place.at_middle)
+    early = comm.copy(from_middle, own, place.pair, place.at_middle)
+    comm.local(from_middle, own, place.at_middle)
+    yield
+    wait_for(outward, place.at_end)
+    late = comm.copy(own, own, place.pair, place.at_end)
+    yield
+    wait_for(early, place.at_middle)
+    wait_for(late, place.at_end)
+    yield
+
+
+def sum_line_first(comm, place, land, source, target, start, count):
+    half = count // 2
+    whole, from_middle, from_pair = land.take(count), land.take(half), land.take(half)
+    all_rows = rows_at(source, start, count)
+    mine, theirs = place.z // 2, 1 - place.z // 2
+    own, rest = rows_at(target, start + mine * half, half), rows_at(target, start + theirs * half, half)
+    inward = comm.copy(all_rows, whole, place.inward, place.at_end)
+    yield
+
+    @pl.when(place.at_middle)
+    def _():
+        inward.wait_recv()
+        whole[...] = whole[...] + all_rows[...]
+
+    across = comm.copy(rows_at(whole, theirs * half, half), from_middle, place.inward, place.at_middle)
+    yield
+
+    @pl.when(place.at_middle)
+    def _():
+        across.wait_recv()
+        from_middle[...] = from_middle[...] + rows_at(whole, mine * half, half)[...]
+
+    paired = comm.copy(from_middle, from_pair, place.pair, place.at_middle)
+    yield
+
+    @pl.when(place.at_middle)
+    def _():
+        paired.wait_recv()
+        from_pair[...] = from_pair[...] + from_middle[...]
+
+    back = comm.copy(from_pair, own, place.inward, place.at_middle)
+    outward = comm.copy(from_pair, own, place.outward, place.at_middle)
+    comm.local(from_pair, own, place.at_middle)
+    yield
+    wait_for(back, place.at_middle)
+    last = comm.copy(rest, rest, place.outward, place.at_middle)
+    yield
+    wait_for(outward, place.at_end)
+    wait_for(last, place.at_end)
+    yield
+
+
+class Crew:
+    def __init__(self):
+        self.waiting = []
+
+    def add(self, one, delay=0):
+        self.waiting.append([one, delay])
+
+    def advance(self):
+        left = []
+        for entry in self.waiting:
+            if entry[1] > 0:
+                entry[1] -= 1
+                left.append(entry)
+                continue
+            try:
+                next(entry[0])
+                left.append(entry)
+            except StopIteration:
+                pass
+        self.waiting = left
+
+    def drain(self):
+        while self.waiting:
+            self.advance()
+
+
+def split(value):
+    high = value.astype(jnp.bfloat16)
+    return high, (value - high.astype(jnp.float32)).astype(jnp.bfloat16)
+
+
+def dot(left, right, dims):
+    return lax.dot_general(left, right, (dims, ((), ())), preferred_element_type=jnp.float32)
+
+
+def dot_three(left, right, dims):
+    return dot(left[0], right[0], dims) + (dot(left[0], right[1], dims) + dot(left[1], right[0], dims))
+
+
+PLAIN, BOTH_LAST, BOTH_FIRST = ((1,), (0,)), ((1,), (1,)), ((0,), (0,))
+
+
+def product(left, right, dims=PLAIN):
+    return dot_three(split(left), split(right), dims)
+
+
+def beside(value):
+    high, low = split(value)
+    return jnp.concatenate([high, high, low], 1)
+
+
+def against(value):
+    high, low = split(value)
+    return jnp.concatenate([high, low, high], 0)
+
+
+def unit_rows(rows):
+    centered = rows - jnp.mean(rows, -1, keepdims=True)
+    inverse = lax.rsqrt(jnp.mean(centered * centered, -1, keepdims=True) + EPSILON)
+    return centered * inverse, inverse
+
+
+def longer_first(lengths):
+    return jnp.where(lengths[1] > lengths[0], 1, 0).astype(jnp.int32)
+
+
+def head_lanes(head, base=0):
+    return slice(base + head * HSIZE, base + (head + 1) * HSIZE)
+
+
+class Spread:
+    def __init__(self, comm, place, part, ends, upward=True, own=None):
+        self.comm, self.place, self.part, self.ends = comm, place, part, ends
+        self.own = own or (lambda half: part(place.seq, half))
+        z, y = place.z, place.y
+        self.rank = z if upward else ends - 1 - z
+        self.inside = z < ends
+        self.more = self.inside & ((z < ends - 1) if upward else (z > 0))
+        self.leads = (y == 0) if upward else (y == 1)
+        self.next = (place.seq + (2 if upward else -2), place.head)
+        self.sign = 1 if upward else -1
+        self.up = {}
+        self.over = {}
+
+    def block(self, level, slot):
+        place = self.place
+        side = place.y if slot == 0 else place.other
+        return 2 * (place.z - self.sign * level) + side
+
+    def begin(self):
+        comm, place, part = self.comm, self.place, self.part
+        near, far = part(place.seq, place.y), part(place.seq, place.other)
+        mine = self.own(place.y)
+        self.lend = comm.copy(self.own(place.other), far, place.pair, self.inside & (self.more | self.leads))
+        self.up[1, 0] = comm.copy(mine, near, self.next, self.more)
+        self.give = comm.copy(mine, near, place.pair, self.inside & self.leads)
+
+    def pass_pair(self):
+        comm, place, part = self.comm, self.place, self.part
+        follows = jnp.logical_not(self.leads)
+        wait_for(self.lend, self.inside & (self.more | follows))
+        lent = part(self.block(0, 1), place.y)
+        self.up[1, 1] = comm.copy(lent, lent, self.next, self.more)
+
+    def have_pair(self):
+        wait_for(self.give, self.inside & jnp.logical_not(self.leads))
+
+    def pass_level(self, level):
+        comm, place, part = self.comm, self.place, self.part
+        here = self.inside & (self.rank >= level)
+        for slot in range(2):
+            half = part(self.block(level, slot), place.y)
+            wait_for(self.up[level, slot], here)
+            if level < LINE - 1:
+                self.up[level + 1, slot] = comm.copy(half, half, self.next, here & self.more)
+            self.over[level, slot] = comm.copy(half, half, place.pair, here)
+
+    def have_level(self, level):
+        here = self.inside & (self.rank >= level)
+        for slot in range(2):
+            wait_for(self.over[level, slot], here)
+
+
+def greet(partners):
+    barrier = pltpu.get_barrier_semaphore()
+    count = jnp.int32(0)
+    for device, when in partners:
+        def tell(device=device):
+            pl.semaphore_signal(barrier, inc=1, device_id=device, device_id_type=MESH)
+
+        if when is None:
+            tell()
+            count = count + 1
+        else:
+            pl.when(when)(tell)
+            count = count + when.astype(jnp.int32)
+    pl.semaphore_wait(barrier, count)
+
+
+def line_partners(place):
+    return [
+        (place.pair, None),
+        ((place.seq + 2, place.head), place.z < LINE - 1),
+        ((place.seq - 2, place.head), place.z > 0),
+    ]
+
+
+def head_partners(place):
+    return [(place.sibling, None), (place.facing, None)]
+
+
+def step_partners(place):
+    return [
+        ((place.seq + 1, place.head), (place.y == 1) & (place.z < LINE - 1)),
+        ((place.seq - 1, place.head), (place.y == 0) & (place.z > 0)),
+    ]
+
+
+def front_kernel(
+    ends,
+    lengths,
+    inputs,
+    gain,
+    shift,
+    query_weight,
+    key_weight,
+    value_weight,
+    query_kernel,
+    key_kernel,
+    value_kernel,
+    output_weight,
+    keyvals,
+    queries,
+    raw,
+    attended,
+    attended_turned,
+    log_total,
+    weights,
+    joined,
+    halo,
+    rows_high,
+    rows_low,
+    query_cat,
+    highest,
+    summed,
+    weighted,
+    send_sems,
+    recv_sems,
+):
+    place = Place()
+    comm = Comm(send_sems, recv_sems)
+    sequences, rows, model = inputs.shape
+    channels = query_weight.shape[1]
+    heads = channels // HSIZE
+    edge = halo.shape[1]
+    first = longer_first(lengths)
+    order = (first, 1 - first)
+    greet(line_partners(place) + head_partners(place) + step_partners(place))
+    rim = comm.copy(
+        inputs.at[:, pl.ds(rows - edge, edge)],
+        halo,
+        (place.seq + 1, place.head),
+        place.seq < 2 * LINE - 1,
+    )
+    own_weight = rows_at(weights, place.head * channels, channels)
+    own_weight[...] = output_weight[...]
+    to_sibling = comm.copy(own_weight, own_weight, place.sibling)
+    to_facing = comm.copy(own_weight, own_weight, place.facing)
+
+    def normal(value):
+        return unit_rows(value)[0] * gain[...] + shift[...]
+
+    for i in range(sequences):
+        high, low = split(normal(inputs[order[i]]))
+        rows_high[pl.ds(i * rows, rows)] = high
+        rows_low[pl.ds(i * rows, rows)] = low
+    wait_for(rim, place.seq > 0)
+    inner = (place.seq > 0).astype(jnp.float32)
+    rim_rows = jnp.concatenate([normal(halo[order[i]]) for i in range(sequences)], 0)
+    rim_split = split(rim_rows)
+    for k, weight in enumerate((query_weight, key_weight, value_weight)):
+        parts = split(weight[...])
+        whole = dot_three((rows_high[...], rows_low[...]), parts, PLAIN)
+        before = dot_three(rim_split, parts, PLAIN) * inner
+        for i in range(sequences):
+            raw[k, i, pl.ds(0, edge)] = before[i * edge : (i + 1) * edge]
+            raw[k, i, pl.ds(edge, rows)] = whole[i * rows : (i + 1) * rows]
+
+    def convolved(k, i, kernel):
+        return (
+            kernel[0:1] * raw[k, i, pl.ds(edge, rows)]
+            + kernel[1:2] * raw[k, i, pl.ds(edge - 1, rows)]
+            + kernel[2:3] * raw[k, i, pl.ds(edge - 2, rows)]
+        )
+
+    spreads = []
+    for i in range(sequences):
+        own = keyvals.at[place.seq, i]
+        own[:, 0:channels] = convolved(1, i, key_kernel)
+        own[:, channels : 2 * channels] = convolved(2, i, value_kernel)
+
+        def part(block, half, i=i):
+            return keyvals.at[block, i, pl.ds(pl.multiple_of(half * (rows // 2), 8), rows // 2)]
+
+        spreads.append(Spread(comm, place, part, ends[i]))
+        spreads[i].begin()
+    for i in range(sequences):
+        query = convolved(0, i, query_kernel).T
+        queries[i] = query
+        for head in range(heads):
+            query_cat[i, head] = against(query[head_lanes(head)] * HSIZE ** (-0.5))
+    to_facing.wait_recv()
+    theirs = rows_at(weights, place.facing[1] * channels, channels)
+    to_last = comm.copy(theirs, theirs, place.sibling)
+
+    def attend(i, block, diagonal):
+        own = keyvals.at[block, i]
+        for head in range(heads):
+            scores = dot(beside(own[:, head_lanes(head)]), query_cat[i, head], PLAIN)
+            lane = pl.ds(head, 1)
+            if diagonal:
+                key_pos = lax.broadcasted_iota(jnp.int32, scores.shape, 0)
+                query_pos = lax.broadcasted_iota(jnp.int32, scores.shape, 1)
+                scores = jnp.where(key_pos <= query_pos, scores, NEGATIVE)
+                high = jnp.max(scores, 0, keepdims=True)
+            else:
+                old = highest[i, lane]
+                high = jnp.maximum(old, jnp.max(scores, 0, keepdims=True))
+            powers = jnp.exp(scores - high)
+            total = jnp.sum(powers, 0, keepdims=True)
+            power_high, power_low = split(powers)
+            value_high, value_low = split(own[:, head_lanes(head, channels)])
+            both = dot(jnp.concatenate([value_high, value_low], 1), power_high, BOTH_FIRST)
+            term = both[:HSIZE] + both[HSIZE:] + dot(value_high, power_low, BOTH_FIRST)
+            at = pl.ds(head * HSIZE, HSIZE)
+            if diagonal:
+                summed[i, lane] = total
+                weighted[i, at] = term
+            else:
+                scale = jnp.exp(old - high)
+                summed[i, lane] = summed[i, lane] * scale + total
+                weighted[i, at] = weighted[i, at] * scale + term
+            highest[i, lane] = high
+
+    def here(i):
+        return place.z < ends[i]
+
+    def both(body):
+        def step(i, carry):
+            body(i)
+            return carry
+
+        lax.fori_loop(0, sequences, step, 0)
+
+    for k, weight in enumerate((query_weight, key_weight, value_weight)):
+        joined[k * channels : (k + 1) * channels] = weight[...].T
+    for spread in spreads:
+        spread.pass_pair()
+    both(lambda i: attend(i, place.seq, True))
+    for spread in spreads:
+        spread.have_pair()
+
+    for level in range(LINE):
+        if level:
+            for spread in spreads:
+                spread.pass_level(level)
+            for spread in spreads:
+                spread.have_level(level)
+
+        def blocks(k, carry, level=level):
+            i, slot = k // 2, k % 2
+            block = 2 * (place.z - level) + slot
+            limit = jnp.where(i == 0, ends[0], ends[1])
+            if level:
+                wanted = (place.z >= level) & (place.z < limit)
+            else:
+                wanted = (slot == 0) & (place.y == 1) & (place.z < limit)
+
+            @pl.when(wanted)
+            def _():
+                attend(i, block, False)
+
+            return carry
+
+        lax.fori_loop(0, 2 * sequences, blocks, 0)
+
+    for i in range(sequences):
+        live = jnp.minimum(lengths[order[i]] - place.seq * rows, rows)
+        alive = (lax.broadcasted_iota(jnp.int32, (1, rows), 1) < live).astype(jnp.float32)
+        for head in range(heads):
+            at = pl.ds(head * HSIZE, HSIZE)
+            total = summed[i, pl.ds(head, 1)]
+            weighted[i, at] = weighted[i, at] * (alive / total)
+            log_total[i, pl.ds(head, 1)] = highest[i, pl.ds(head, 1)] + jnp.log(total)
+        attended_turned[i] = weighted[i]
+        attended[:, i * channels : (i + 1) * channels] = weighted[i].T
+    to_sibling.wait_recv()
+    to_last.wait_recv()
+    comm.finish()
+
+
+def front(ends, lengths, inputs, gain, shift, weights, kernels, output_weight):
+    sequences, rows, model = inputs.shape
+    channels = weights[0].shape[1]
+    heads = channels // HSIZE
+    blocks = lax.axis_size("seq")
+    groups = lax.axis_size("head")
+    edge = 8
+    vmem = pl.BlockSpec(memory_space=pltpu.VMEM)
+
+    def f32(*shape):
+        return jax.ShapeDtypeStruct(shape, jnp.float32)
+
+    copies = 64
+    return pl.pallas_call(
+        functools.partial(front_kernel, ends),
+        out_shape=[
+            f32(blocks, sequences, rows, 2 * channels),
+            f32(sequences, channels, rows),
+            f32(3, sequences, rows + edge, channels),
+            f32(rows, sequences * channels),
+            f32(sequences, channels, rows),
+            f32(sequences, 8, rows),
+            f32(groups * channels, model),
+            f32(3 * channels, model),
+        ],
+        in_specs=[pl.BlockSpec(memory_space=pltpu.SMEM)] + [vmem] * 10,
+        out_specs=[vmem] * 8,
+        scratch_shapes=[
+            pltpu.VMEM((sequences, edge, model), jnp.float32),
+            pltpu.VMEM((sequences * rows, model), jnp.bfloat16),
+            pltpu.VMEM((sequences * rows, model), jnp.bfloat16),
+            pltpu.VMEM((sequences, heads, 3 * HSIZE, rows), jnp.bfloat16),
+            pltpu.VMEM((sequences, 8, rows), jnp.float32),
+            pltpu.VMEM((sequences, 8, rows), jnp.float32),
+            pltpu.VMEM((sequences, channels, rows), jnp.float32),
+            pltpu.SemaphoreType.DMA((copies,)),
+            pltpu.SemaphoreType.DMA((copies,)),
+        ],
+        compiler_params=pltpu.CompilerParams(
+            collective_id=1, has_side_effects=True, vmem_limit_bytes=60 * 2**20
+        ),
+        name="front",
+    )(lengths, inputs, gain[None], shift[None], *weights, *kernels, output_weight)
+
+
+class HeadSum:
+    def __init__(self, comm, place, partial, from_sibling, from_facing, rows, pieces=4):
+        self.comm, self.place, self.partial = comm, place, partial
+        self.from_sibling, self.from_facing = from_sibling, from_facing
+        self.rows, self.pieces = rows, pieces
+        self.size = rows // pieces
+        self.near = rows_at(partial, place.core * rows, rows)
+
+    def lend(self):
+        far = rows_at(self.partial, (1 - self.place.core) * self.rows, self.rows)
+        self.lent = self.comm.copy(far, self.from_sibling, self.place.sibling)
+
+    def chip(self):
+        self.lent.wait_recv()
+        self.near[...] = self.near[...] + self.from_sibling[...]
+        self.sent = []
+        for p in range(self.pieces):
+            at = pl.ds(p * self.size, self.size)
+            self.sent.append(self.comm.copy(self.near.at[at], self.from_facing.at[at], self.place.facing))
+
+    def piece(self, p):
+        self.sent[p].wait_recv()
+        at = pl.ds(p * self.size, self.size)
+        return self.near[at] + self.from_facing[at]
+
+
+def norm_back(grad, gain, unit, inverse):
+    scaled = grad * gain
+    return inverse * (
+        scaled - jnp.mean(scaled, -1, keepdims=True) - unit * jnp.mean(scaled * unit, -1, keepdims=True)
+    )
+
+
+def spread_steps(spreads):
+    for spread in spreads:
+        spread.begin()
+    yield
+    for spread in spreads:
+        spread.pass_pair()
+    yield
+    for level in range(1, LINE):
+        for spread in spreads:
+            spread.pass_level(level)
+        yield
+
+
+TILE = 256
+
+
+def tiles(width, body):
+    def step(j, carry):
+        body(pl.ds(pl.multiple_of(j * TILE, TILE), TILE))
+        return carry
+
+    lax.fori_loop(0, width // TILE, step, 0)
+
+
+def down_rows(value):
+    return jnp.sum(value, 0, keepdims=True)
+
+
+def allowed_from(shape, offset):
+    key_pos = lax.broadcasted_iota(jnp.int32, shape, 0)
+    query_pos = lax.broadcasted_iota(jnp.int32, shape, 1)
+    return key_pos <= query_pos + offset
+
+
+def back_kernel(
+    ends,
+    plan,
+    lengths,
+    inputs,
+    cotangent,
+    attended,
+    attended_turned,
+    queries,
+    log_total,
+    output_weight,
+    output_bias,
+    first_gain,
+    first_shift,
+    second_gain,
+    second_shift,
+    hidden_bias,
+    outer_bias,
+    query_kernel,
+    key_kernel,
+    value_kernel,
+    keyvals,
+    weights,
+    inner_weight,
+    outer_weight,
+    joined,
+    raw_far,
+    result,
+    grad_inputs,
+    outer_out,
+    inner_out,
+    rest_out,
+    late_out,
+    all_queries,
+    all_grads,
+    weight_a,
+    weight_b,
+    weight_c,
+    raw,
+    groups,
+    normed_two,
+    active,
+    grad_hidden,
+    grad_normed,
+    from_sibling,
+    from_facing,
+    grad_outer,
+    grad_inner,
+    grad_rest,
+    land_ref,
+    key_slots,
+    own_keys,
+    query_slots,
+    grad_slots,
+    query_cat,
+    grad_cat,
+    key_cat,
+    value_cat,
+    grad_att,
+    grad_query,
+    grad_keyval,
+    grad_conv,
+    late_from,
+    late_all,
+    send_sems,
+    recv_sems,
+    local_sems,
+    slot_sems,
+):
+    place = Place()
+    comm = Comm(send_sems, recv_sems, local_sems)
+    land = Land(land_ref)
+    crew = Crew()
+    sequences, rows, model = inputs.shape
+    channels = output_weight.shape[0]
+    heads = channels // HSIZE
+    hidden_units = hidden_bias.shape[1]
+    tokens = sequences * rows
+    z, y, seq, core = place.z, place.y, place.seq, place.core
+    first = longer_first(lengths)
+    order = (first, 1 - first)
+    devices = 2 * LINE
+    column = [((lax.rem(seq + k, devices), place.head), None) for k in range(1, devices)]
+    greet(column + head_partners(place))
+
+    load_a = comm.local(weights, weight_a, keep=False)
+    load_b = comm.local(inner_weight, weight_b, keep=False)
+    load_c = comm.local(outer_weight, weight_c, keep=False)
+    load_raw = comm.local(raw_far, raw, keep=False)
+    load_own = [comm.local(keyvals.at[seq, i], own_keys.at[i], keep=False) for i in range(sequences)]
+    keep_query = [comm.local(queries.at[i], all_queries.at[seq, i], keep=False) for i in range(sequences)]
+
+    to_sibling = comm.copy(attended, groups.at[place.head], place.sibling)
+    to_facing = comm.copy(attended, groups.at[place.head], place.facing)
+
+    def query_part(block, half, i):
+        return all_queries.at[block, i, pl.ds(pl.multiple_of(half * (channels // 2), 8), channels // 2)]
+
+    def grad_part(block, half, i):
+        size = grad_att.shape[1] // 2
+        return all_grads.at[block, i, pl.ds(pl.multiple_of(half * size, 8), size)]
+
+    def query_own(half, i):
+        return queries.at[i, pl.ds(pl.multiple_of(half * (channels // 2), 8), channels // 2)]
+
+    def grad_own(half, i):
+        size = grad_att.shape[1] // 2
+        return grad_att.at[i, pl.ds(pl.multiple_of(half * size, 8), size)]
+
+    query_spreads = [
+        Spread(
+            comm,
+            place,
+            functools.partial(query_part, i=i),
+            ends[i],
+            False,
+            functools.partial(query_own, i=i),
+        )
+        for i in range(sequences)
+    ]
+    grad_spreads = [
+        Spread(
+            comm,
+            place,
+            functools.partial(grad_part, i=i),
+            ends[i],
+            False,
+            functools.partial(grad_own, i=i),
+        )
+        for i in range(sequences)
+    ]
+    crew.add(spread_steps(query_spreads))
+    crew.advance()
+
+    def chunk(i):
+        return pl.ds(i * rows, rows)
+
+    def add_group(ref, weight_ref, total, begin):
+        parts = split(weight_ref[...])
+        for i in range(sequences):
+            piece = split(ref[:, i * channels : (i + 1) * channels])
+            term = dot_three(piece, parts, PLAIN)
+            total[chunk(i)] = term if begin else total[chunk(i)] + term
+
+    add_group(attended, output_weight, grad_inputs, True)
+    crew.advance()
+    load_a.wait()
+
+    def group_weight(group):
+        return rows_at(weight_a, group * channels, channels)
+
+    sibling, facing = place.sibling[1], place.facing[1]
+    last = facing + 1 - 2 * (facing % 2)
+    to_sibling.wait_recv()
+    add_group(groups.at[sibling], group_weight(sibling), grad_inputs, False)
+    to_facing.wait_recv()
+    onward = comm.copy(groups.at[facing], groups.at[facing], place.sibling)
+    add_group(groups.at[facing], group_weight(facing), result, True)
+    crew.advance()
+    onward.wait_recv()
+    add_group(groups.at[last], group_weight(last), result, False)
+
+    for i in range(sequences):
+        result[chunk(i)] = inputs[order[i]] + output_bias[...] + (grad_inputs[chunk(i)] + result[chunk(i)])
+        normed_two[chunk(i)] = unit_rows(result[chunk(i)])[0] * second_gain[...] + second_shift[...]
+    load_b.wait()
+    load_c.wait()
+
+    def cot_columns(columns):
+        return jnp.concatenate([cotangent[order[i], :, columns] for i in range(sequences)], 0)
+
+    normed_parts = split(normed_two[...])
+    cot_parts = split(jnp.concatenate([cotangent[order[i]] for i in range(sequences)], 0))
+
+    def hidden_tile(columns):
+        hidden = dot_three(normed_parts, split(weight_b[:, columns]), PLAIN) + hidden_bias[:, columns]
+        rectified = jnp.maximum(hidden, 0.0)
+        grad_active = dot_three(cot_parts, split(weight_c[columns]), BOTH_LAST)
+        grad = grad_active * (2.0 * rectified)
+        active[:, columns] = rectified * rectified
+        grad_hidden[:, columns] = grad
+        grad_rest[4 * channels + 2 : 4 * channels + 3, columns] = down_rows(grad)
+
+    tiles(hidden_units, hidden_tile)
+    crew.advance()
+
+    def grad_normed_chunk(which):
+        at = pl.ds(pl.multiple_of(which * rows, rows), rows)
+        parts = split(grad_hidden[at])
+
+        def tile(columns):
+            grad_normed[at, columns] = dot_three(parts, split(weight_b[columns]), BOTH_LAST)
+
+        tiles(model, tile)
+
+    second_sum = HeadSum(comm, place, grad_normed, from_sibling.at[0], from_facing.at[0], rows)
+    grad_normed_chunk(1 - core)
+    second_sum.lend()
+    grad_normed_chunk(core)
+    second_sum.chip()
+
+    active_parts = split(active[...])
+
+    def outer_tile(columns):
+        grad_outer[:, columns] = dot_three(active_parts, split(cot_columns(columns)), BOTH_FIRST)
+
+    tiles(model, outer_tile)
+    for pair_first, which, start, count in plan:
+        if which == 0:
+            crew.add(sum_pair_first(comm, place, land, grad_outer, outer_out, start, count))
+    crew.advance()
+
+    normed_parts = split(normed_two[...])
+
+    def inner_tile(columns):
+        grad_inner[:, columns] = dot_three(normed_parts, split(grad_hidden[:, columns]), BOTH_FIRST)
+
+    tiles(hidden_units, inner_tile)
+    for pair_first, which, start, count in plan:
+        if which == 1:
+            crew.add(sum_line_first(comm, place, land, grad_inner, inner_out, start, count))
+    crew.advance()
+
+    outer_term = weight_a.at[pl.ds(0, tokens)]
+
+    def outer_term_tile(columns):
+        outer_term[:, columns] = dot_three(active_parts, split(weight_c[:, columns]), PLAIN)
+
+    tiles(model, outer_term_tile)
+    load_joined = comm.local(joined, weight_c.at[pl.ds(0, 3 * channels)], keep=False)
+
+    late_out[...] = jnp.zeros_like(late_out)
+    swaps = []
+
+    def own_piece(p, size):
+        return pl.ds(pl.multiple_of(core * rows + p * size, 8), size)
+
+    for p in range(second_sum.pieces):
+        at = own_piece(p, second_sum.size)
+        incoming = second_sum.piece(p)
+        unit, inverse = unit_rows(result[at])
+        through = norm_back(incoming, second_gain[...], unit, inverse)
+        here = pl.ds(p * second_sum.size, second_sum.size)
+        cot = jnp.where(core == 0, cotangent[order[0], here], cotangent[order[1], here])
+        grad_inputs[at] = cot + through
+        late_out[2:3] = late_out[2:3] + down_rows(incoming * unit)
+        late_out[3:4] = late_out[3:4] + down_rows(incoming)
+        swaps.append(comm.copy(grad_inputs.at[at], grad_inputs.at[at], place.sibling))
+    result_sum = HeadSum(comm, place, outer_term, from_sibling.at[1], from_facing.at[1], rows)
+    result_sum.lend()
+    for made in swaps:
+        made.wait_recv()
+
+    weight_parts = split(output_weight[...])
+    grad_att[:, channels:] = jnp.zeros((sequences, grad_att.shape[1] - channels, rows), jnp.float32)
+    for i in range(sequences):
+        live = jnp.minimum(lengths[order[i]] - seq * rows, rows)
+        alive = (lax.broadcasted_iota(jnp.int32, (1, rows), 1) < live).astype(jnp.float32)
+        grad = dot_three(weight_parts, split(grad_inputs[chunk(i)]), BOTH_LAST) * alive
+        grad_att[i, 0:channels] = grad
+        both = grad * attended_turned[i]
+        for head in range(heads):
+            at = channels + head
+            grad_att[i, at : at + 1] = log_total[i, head : head + 1]
+            grad_att[i, at + heads : at + heads + 1] = down_rows(both[head_lanes(head)])
+    keep_grad = [comm.local(grad_att.at[i], all_grads.at[seq, i], keep=False) for i in range(sequences)]
+    for spread in grad_spreads:
+        spread.begin()
+    result_sum.chip()
+    for i in range(sequences):
+        for head in range(heads):
+            query_cat[i, head] = against(queries[i, head_lanes(head)] * HSIZE ** (-0.5))
+            grad_cat[i, head] = against(grad_att[i, head_lanes(head)])
+    output_grad = jnp.zeros((channels, model), jnp.float32)
+    for i in range(sequences):
+        output_grad = output_grad + dot_three(split(attended_turned[i]), split(grad_inputs[chunk(i)]), PLAIN)
+    grad_rest[0:channels] = output_grad
+    base = 4 * channels
+    grad_rest[base : base + 1] = down_rows(grad_inputs[...])
+    outer_row = jnp.zeros((1, model), jnp.float32)
+    for i in range(sequences):
+        outer_row = outer_row + down_rows(cotangent[order[i]])
+    grad_rest[base + 1 : base + 2] = outer_row
+    for pair_first, which, start, count in plan:
+        if which == 2 and start < channels:
+            make = sum_pair_first if pair_first else sum_line_first
+            crew.add(make(comm, place, land, grad_rest, rest_out, start, count))
+    for spread in grad_spreads:
+        spread.pass_pair()
+    crew.advance()
+
+    grad_query[...] = jnp.zeros_like(grad_query)
+    grad_keyval[...] = jnp.zeros_like(grad_keyval)
+
+    def query_side(i):
+        count = jnp.where(z < ends[i], seq + 1, 0)
+
+        def load(slot, block):
+            return pltpu.make_async_copy(keyvals.at[block, i], key_slots.at[slot], slot_sems.at[slot])
+
+        pl.when(count > 0)(lambda: load(0, seq).start())
+
+        def step(t, carry):
+            slot = lax.rem(t, 2)
+            load(slot, seq - t).wait()
+            pl.when(t + 1 < count)(lambda: load(1 - slot, seq - t - 1).start())
+            block = key_slots.at[slot]
+            for head in range(heads):
+                key_high, key_low = split(block[:, head_lanes(head)])
+                scores = dot(jnp.concatenate([key_high, key_high, key_low], 1), query_cat[i, head], PLAIN)
+                at = channels + head
+                scores = scores - grad_att[i, at : at + 1]
+                powers = jnp.exp(jnp.where(allowed_from(scores.shape, t * rows), scores, NEGATIVE))
+                slopes = dot(beside(block[:, head_lanes(head, channels)]), grad_cat[i, head], PLAIN)
+                slopes = powers * (slopes - grad_att[i, at + heads : at + heads + 1])
+                high, low = split(slopes)
+                both = dot(jnp.concatenate([key_high, key_low], 1), high, BOTH_FIRST)
+                term = both[:HSIZE] + both[HSIZE:] + dot(key_high, low, BOTH_FIRST)
+                grad_query[i, head_lanes(head)] = grad_query[i, head_lanes(head)] + term
+            return carry
+
+        lax.fori_loop(0, count, step, 0)
+
+    def key_side(i, offset, query_ref, grad_ref):
+        for head in range(heads):
+            lanes = head_lanes(head)
+            query_high, query_low = split(query_ref[lanes] * HSIZE ** (-0.5))
+            grad_high, grad_low = split(grad_ref[lanes])
+            scores = dot(
+                key_cat[i, head, :, 0 : 3 * HSIZE],
+                jnp.concatenate([query_high, query_low, query_high], 0),
+                PLAIN,
+            )
+            at = channels + head
+            scores = scores - grad_ref[at : at + 1]
+            powers = jnp.exp(jnp.where(allowed_from(scores.shape, offset), scores, NEGATIVE))
+            slopes = dot(
+                value_cat[i, head, :, 0 : 3 * HSIZE],
+                jnp.concatenate([grad_high, grad_low, grad_high], 0),
+                PLAIN,
+            )
+            slopes = powers * (slopes - grad_ref[at + heads : at + heads + 1])
+            for base, (far_high, far_low), value in (
+                (0, (query_high, query_low), slopes),
+                (channels, (grad_high, grad_low), powers),
+            ):
+                high, low = split(value)
+                both = dot(jnp.concatenate([far_high, far_low], 0), high, BOTH_LAST)
+                term = both[:HSIZE] + both[HSIZE:] + dot(far_high, low, BOTH_LAST)
+                where = slice(base + head * HSIZE, base + (head + 1) * HSIZE)
+                grad_keyval[i, where] = grad_keyval[i, where] + term
+
+    def key_level(level, pairs):
+        items = [(i, slot) for i in range(sequences) for slot in range(2)]
+
+        def inside(i):
+            return z + level < jnp.where(i == 0, ends[0], ends[1])
+
+        def wanted(t):
+            i, slot = t // 2, t % 2
+            if level:
+                return inside(i)
+            if pairs:
+                return inside(i) & (slot == 1) & (y == 0)
+            return inside(i) & (slot == y)
+
+        def loads(t):
+            i, slot = t // 2, t % 2
+            block = 2 * (z + level) + slot
+            return (
+                pltpu.make_async_copy(all_queries.at[block, i], query_slots.at[t], slot_sems.at[2 * t]),
+                pltpu.make_async_copy(all_grads.at[block, i], grad_slots.at[t], slot_sems.at[2 * t + 1]),
+            )
+
+        for t in range(len(items)):
+            @pl.when(wanted(t))
+            def _(t=t):
+                for made in loads(t):
+                    made.start()
+
+        def step(t, carry):
+            @pl.when(wanted(t))
+            def _():
+                for made in loads(t):
+                    made.wait()
+                i, slot = t // 2, t % 2
+                offset = (2 * (z + level) + slot - seq) * rows
+                key_side(i, offset, query_slots.at[t], grad_slots.at[t])
+
+            return carry
+
+        lax.fori_loop(0, len(items), step, 0)
+
+    query_side(0)
+    crew.advance()
+    for spread in grad_spreads:
+        spread.pass_level(1)
+    query_side(1)
+    crew.advance()
+    for p in range(result_sum.pieces):
+        at = own_piece(p, result_sum.size)
+        result[at] = result[at] + outer_bias[...] + result_sum.piece(p)
+        swaps.append(comm.copy(result.at[at], result.at[at], place.sibling))
+    for i in range(sequences):
+        load_own[i].wait()
+        for head in range(heads):
+            key_cat[i, head, :, 0 : 3 * HSIZE] = beside(own_keys[i, :, head_lanes(head)])
+            value_cat[i, head, :, 0 : 3 * HSIZE] = beside(own_keys[i, :, head_lanes(head, channels)])
+        keep_query[i].wait()
+        keep_grad[i].wait()
+    key_level(0, False)
+    crew.advance()
+    for spread in grad_spreads:
+        spread.pass_level(2)
+    for spread in query_spreads + grad_spreads:
+        spread.have_pair()
+    key_level(0, True)
+    crew.advance()
+    for level in range(1, LINE):
+        if level == 2:
+            for spread in grad_spreads:
+                spread.pass_level(3)
+        for spread in query_spreads + grad_spreads:
+            spread.have_level(level)
+        key_level(level, False)
+        crew.advance()
+
+    edge = grad_conv.shape[2] - rows
+    for i in range(sequences):
+        grad_conv[0, i, pl.ds(0, rows)] = (grad_query[i] * HSIZE ** (-0.5)).T
+        grad_conv[1, i, pl.ds(0, rows)] = grad_keyval[i, 0:channels].T
+        grad_conv[2, i, pl.ds(0, rows)] = grad_keyval[i, channels : 2 * channels].T
+
+    @pl.when(seq == devices - 1)
+    def _():
+        grad_conv[:, :, pl.ds(rows, edge)] = jnp.zeros((3, sequences, edge, channels), jnp.float32)
+
+    before = (seq - 1, place.head)
+    rim = comm.copy(
+        grad_conv.at[:, :, pl.ds(0, edge)], grad_conv.at[:, :, pl.ds(rows, edge)], before, seq > 0
+    )
+    load_raw.wait()
+    base = 4 * channels + 3
+    grad_rest[base : base + 13] = jnp.zeros((13, model), jnp.float32)
+    for k in range(3):
+        for j in range(3):
+            total = jnp.zeros((1, channels), jnp.float32)
+            for i in range(sequences):
+                total = total + down_rows(grad_conv[k, i, pl.ds(0, rows)] * raw[k, i, pl.ds(edge - j, rows)])
+            grad_rest[base + j : base + j + 1, k * channels : (k + 1) * channels] = total
+    wait_for(rim, seq < devices - 1)
+    for k, kernel in enumerate((query_kernel, key_kernel, value_kernel)):
+        for i in range(sequences):
+            grad_hidden[chunk(i), k * channels : (k + 1) * channels] = (
+                kernel[0:1] * grad_conv[k, i, pl.ds(0, rows)]
+                + kernel[1:2] * grad_conv[k, i, pl.ds(1, rows)]
+                + kernel[2:3] * grad_conv[k, i, pl.ds(2, rows)]
+            )
+    load_joined.wait()
+
+    def first_chunk(which):
+        at = pl.ds(pl.multiple_of(which * rows, rows), rows)
+        parts = split(grad_hidden[at, 0 : 3 * channels])
+
+        def tile(columns):
+            active[at, columns] = dot_three(parts, split(weight_c[0 : 3 * channels, columns]), PLAIN)
+
+        tiles(model, tile)
+
+    first_sum = HeadSum(comm, place, active, from_sibling.at[2], from_facing.at[2], rows)
+    first_chunk(1 - core)
+    first_sum.lend()
+    first_chunk(core)
+    first_sum.chip()
+    for i in range(sequences):
+        normed_two[chunk(i)] = unit_rows(inputs[order[i]])[0] * first_gain[...] + first_shift[...]
+    projected_parts = split(grad_hidden[:, 0 : 3 * channels])
+
+    def joined_tile(columns):
+        grad_rest[channels : 4 * channels, columns] = dot_three(
+            projected_parts, split(normed_two[:, columns]), BOTH_FIRST
+        )
+
+    tiles(model, joined_tile)
+    for pair_first, which, start, count in plan:
+        if which == 2 and start >= channels:
+            make = sum_pair_first if pair_first else sum_line_first
+            crew.add(make(comm, place, land, grad_rest, rest_out, start, count))
+    crew.advance()
+    crew.advance()
+
+    pieces = swaps[: second_sum.pieces]
+    for made in pieces:
+        comm.settle(made)
+    returned = []
+    for p in range(first_sum.pieces):
+        at = own_piece(p, first_sum.size)
+        incoming = first_sum.piece(p)
+        here = pl.ds(p * first_sum.size, first_sum.size)
+        rows_in = jnp.where(core == 0, inputs[order[0], here], inputs[order[1], here])
+        unit, inverse = unit_rows(rows_in)
+        grad_inputs[at] = grad_inputs[at] + norm_back(incoming, first_gain[...], unit, inverse)
+        late_out[0:1] = late_out[0:1] + down_rows(incoming * unit)
+        late_out[1:2] = late_out[1:2] + down_rows(incoming)
+        returned.append(comm.copy(grad_inputs.at[at], grad_inputs.at[at], place.sibling))
+    late_sent = comm.copy(late_out, late_from, place.sibling)
+    crew.advance()
+    late_sent.wait_recv()
+    late_all[seq] = late_out[...] + late_from[...]
+    mine = late_all.at[seq]
+    shared = [comm.copy(mine, mine, device) for device, _ in column]
+    crew.drain()
+    for made in swaps[second_sum.pieces :] + returned + shared:
+        made.wait_recv()
+    comm.settle(late_sent)
+    total = late_all[0]
+    for k in range(1, devices):
+        total = total + late_all[k]
+    late_out[...] = total
+    comm.finish()
+
+
+def back(ends, lengths, inputs, cotangent, kept, vectors, kernels, inner_weight, outer_weight, output_weight):
+    keyvals, queries, raw, attended, attended_turned, log_total, weights, joined = kept
+    sequences, rows, model = inputs.shape
+    channels = output_weight.shape[0]
+    heads = channels // HSIZE
+    hidden_units = inner_weight.shape[1]
+    tokens = sequences * rows
+    devices = lax.axis_size("seq")
+    rest_rows = 4 * channels + 16
+    plan = (
+        [(True, 0, k * 192, 192) for k in range(hidden_units // 192)]
+        + [(False, 1, k * 192, 192) for k in range(model // 192)]
+        + [(True, 2, 0, 96), (False, 2, 96, 96)]
+        + [(True, 2, 192, 96), (True, 2, 288, 96), (True, 2, 384, 96)]
+        + [(False, 2, 480, 96), (False, 2, 576, 96), (False, 2, 672, 112)]
+    )
+    land_rows = sum(3 * count // 2 if pair_first else 2 * count for pair_first, _, _, count in plan)
+    vmem = pl.BlockSpec(memory_space=pltpu.VMEM)
+    far = pl.BlockSpec(memory_space=pl.ANY)
+
+    def f32(*shape):
+        return jax.ShapeDtypeStruct(shape, jnp.float32)
+
+    def room(*shape, dtype=jnp.float32):
+        return pltpu.VMEM(shape, dtype)
+
+    edge = 8
+    grad_rows = channels + 16
+    half = functools.partial(room, dtype=jnp.bfloat16)
+    return pl.pallas_call(
+        functools.partial(back_kernel, ends, plan),
+        out_shape=[
+            f32(tokens, model),
+            f32(tokens, model),
+            f32(hidden_units, model),
+            f32(model, hidden_units),
+            f32(rest_rows, model),
+            f32(8, model),
+            f32(devices, sequences, channels, rows),
+            f32(devices, sequences, grad_rows, rows),
+        ],
+        in_specs=[pl.BlockSpec(memory_space=pltpu.SMEM)] + [vmem] * 17 + [far] * 6,
+        out_specs=[vmem] * 2 + [far] * 3 + [vmem] + [far] * 2,
+        scratch_shapes=[
+            room(model, model),
+            room(model, hidden_units),
+            room(hidden_units, model),
+            room(3, sequences, rows + edge, channels),
+            room(4, rows, sequences * channels),
+            room(tokens, model),
+            room(tokens, hidden_units),
+            room(tokens, hidden_units),
+            room(tokens, model),
+            room(3, rows, model),
+            room(3, rows, model),
+            room(hidden_units, model),
+            room(model, hidden_units),
+            room(rest_rows, model),
+            room(land_rows, model),
+            room(2, rows, 2 * channels),
+            room(sequences, rows, 2 * channels),
+            room(2 * sequences, channels, rows),
+            room(2 * sequences, grad_rows, rows),
+            half(sequences, heads, 3 * HSIZE, rows),
+            half(sequences, heads, 3 * HSIZE, rows),
+            half(sequences, heads, rows, 256),
+            half(sequences, heads, rows, 256),
+            room(sequences, grad_rows, rows),
+            room(sequences, channels, rows),
+            room(sequences, 2 * channels, rows),
+            room(3, sequences, rows + edge, channels),
+            room(8, model),
+            room(devices, 8, model),
+            pltpu.SemaphoreType.DMA((256,)),
+            pltpu.SemaphoreType.DMA((256,)),
+            pltpu.SemaphoreType.DMA((64,)),
+            pltpu.SemaphoreType.DMA((4 * sequences,)),
+        ],
+        compiler_params=pltpu.CompilerParams(
+            collective_id=2, has_side_effects=True, vmem_limit_bytes=63 * 2**20
+        ),
+        name="back",
+    )(
+        lengths,
+        inputs,
+        cotangent,
+        attended,
+        attended_turned,
+        queries,
+        log_total,
+        output_weight,
+        *[vector[None] for vector in vectors],
+        *kernels,
+        keyvals,
+        weights,
+        inner_weight,
+        outer_weight,
+        joined,
+        raw,
+    )
+
+
+def shards(
+    inputs,
+    seq_lengths,
+    first_gain,
+    first_shift,
+    query_weight,
+    key_weight,
+    value_weight,
+    query_kernel,
+    key_kernel,
+    value_kernel,
+    output_weight,
+    output_bias,
+    second_gain,
+    second_shift,
+    inner_weight,
+    hidden_layer_bias,
+    outer_weight,
+    outer_bias,
+    cotangent,
+):
+    channels = query_weight.shape[1]
+    kernels = (query_kernel, key_kernel, value_kernel)
+    ends = (LINE, LINE)
+    kept = front(
+        ends,
+        seq_lengths,
+        inputs,
+        first_gain,
+        first_shift,
+        (query_weight, key_weight, value_weight),
+        kernels,
+        output_weight,
+    )
+    result, grad_inputs, grad_outer, grad_inner, rest, late, _, _ = back(
+        ends,
+        seq_lengths,
+        inputs,
+        cotangent,
+        kept,
+        (
+            output_bias,
+            first_gain,
+            first_shift,
+            second_gain,
+            second_shift,
+            hidden_layer_bias,
+            outer_bias,
+        ),
+        kernels,
+        inner_weight,
+        outer_weight,
+        output_weight,
+    )
+    swap = seq_lengths[1] > seq_lengths[0]
+
+    def placed(array):
+        array = array.reshape(inputs.shape)
+        return jnp.where(swap, jnp.flip(array, 0), array)
+
+    vectors = rest[4 * channels :]
+    mixes = vectors[3:6, : 3 * channels]
+    return (
+        placed(result),
+        placed(grad_inputs),
+        late[0],
+        late[1],
+        rest[channels : 2 * channels].T,
+        rest[2 * channels : 3 * channels].T,
+        rest[3 * channels : 4 * channels].T,
+        mixes[:, :channels],
+        mixes[:, channels : 2 * channels],
+        mixes[:, 2 * channels :],
+        rest[:channels],
+        vectors[0],
+        late[2],
+        late[3],
+        grad_inner,
+        vectors[2],
+        grad_outer,
+        vectors[1],
+    )
+
+
 def solution(mesh):
+    lines = mesh.shape["seq"] == 2 * LINE and mesh.shape["head"] == 4
     return jax.shard_map(
-        shards,
+        shards if lines else general_shards,
         mesh=mesh,
         in_specs=(
             P(None, "seq", None),

time: 804 us -> 453 us (0.56)
  waiting for transfers between devices: 464 us -> 0 us
  Pallas kernels: 0 us -> 425 us
  matrix products: 163 us -> 0 us
  blocking collectives: 71.6 us -> 0 us
  other arithmetic: 39 us -> 5.12 us
  local copies, waits for them, and re-layouts: 38.2 us -> 19.7 us
  between operations: 15.2 us -> 2.02 us
    pallas_call x0 -> x2, Pallas kernels: none -> 425 us  [the longest x1 390 us: back(): pl.pallas_call(functools.partial(back_kernel, ends, plan), out_shape=[f32...]
    psum x4 -> x0, waiting for transfers between devices: 329 us -> none  [the longest x1 197 us: shards(): lax.psum((grad_first_gain, grad_first_shift, grad_query_weight, grad_key_...]
    dot_general x20 -> x0, matrix products: 163 us -> none  [the longest x2 21.3 us: pair_terms(): jnp.einsum('sqhe,skhe->shqk', grad_heads, value_heads, precision=EXACT_FL...]
    all_gather x2 -> x0, waiting for transfers between devices: 135 us -> none  [the longest x1 98.2 us: shards(): portion = lax.all_gather(keyvals, 'seq', axis=1, tiled=True)]
    psum x1 -> x0, blocking collectives: 40.3 us -> none  [shards(): lax.psum((grad_first_gain, grad_first_shift, grad_query_weight, grad_key_...]
    all_gather x1 -> x0, blocking collectives: 31.3 us -> none  [shards(): stat_rows = lax.all_gather(row_stats, 'seq', axis=1, tiled=True)]
    reduce_sum x10 -> x0, other arithmetic: 23.9 us -> none  [the longest x2 5.98 us: normalize_back(): jnp.sum(gradient * unit_rows, (0, 1))]
    slice x10 -> x4, local copies, waits for them, and re-layouts: 17.6 us -> 4.27 us  [the longest x1 1.58 us: shards(): vectors[1]]
  transfers between devices with their start and end apart: 8 -> 0, of which waited for: 6 -> 0; matrix products, arithmetic and copies ran while one was open for 9% -> 0% of each run, Pallas kernels for 0% -> 0%
where the time goes in v1:
time: 453 us; the launch traced here: 452 us
  Pallas kernels  425 us (94%)
  local copies, waits for them, and re-layouts  19.7 us (4%)
  other arithmetic  5.12 us (1%)
    pallas_call x1, Pallas kernels, back(): pl.pallas_call(functools.partial(back_kernel, ends, plan), out_shape=[f32...  390 us
    pallas_call x1, Pallas kernels, front(): pl.pallas_call(functools.partial(front_kernel, ends), out_shape=[f32(bloc...  34.4 us
    unnamed x25, local copies, waits for them, and re-layouts  9.94 us

profile of v1, /device:TPU:0, one launch (start us, length us, event | category | flops | bytes accessed | tf_op | source)
XLA Modules:
  0.0 451.6 jit_solution(1036515150780455005)
XLA Ops:
  0.7 0.0 copy-start.3
  0.7 1.3 broadcast_in_dim.23.gain.first_gain
  2.0 1.3 broadcast_in_dim.24.shift.first_shift
  3.3 2.2 copy.37.query_weight
  5.5 2.2 copy.38.key_weight
  7.7 0.0 copy-done.3
  7.7 1.1 copy.39.value_weight
  8.8 0.0 copy-start.5
  8.8 0.0 copy-start.6
  8.8 0.0 copy-start.7
  8.8 0.0 copy-start.8
  8.8 0.0 copy-start.9
  8.9 34.4 %front.1 = (f32[8,2,256,384]{3,2,1,0:T(8,128)}, f32[2,192,256]{2,1,0:T(8,128)}, f32[3,2,264,192]{3,2,1,0:T(8,128)}, f32[256,384]{1,0:T(8,128)}, f32[2,192,256]{2...) custom-call(s32[2]{0:T(128)} %lengths.3, f32[2,256,768]{2,1,0:T(8,128)} %inputs.3, ...), custom_call_target="tpu_custom_call" | custom-call | tf_op jit(solution)/shard_map/front/pallas_call | solution.py:823
  43.2 0.0 copy-done.5
  43.2 0.6 broadcast_in_dim.25.output_bias
  43.8 0.0 copy-done.6
  43.8 0.6 broadcast_in_dim.26.second_gain
  44.4 0.0 copy-done.7
  44.4 0.6 broadcast_in_dim.27.second_shift
  45.0 0.0 copy-done.8
  45.0 0.6 broadcast_in_dim.28.hidden_bias
  45.6 0.0 copy-done.9
  45.6 0.6 broadcast_in_dim.29.outer_bias
  46.2 0.0 copy-start.4
  46.2 390.4 %back.1 = (f32[512,768]{1,0:T(8,128)}, f32[512,768]{1,0:T(8,128)}, f32[768,768]{1,0:T(8,128)}, f32[768,768]{1,0:T(8,128)}, f32[784,768]{1,0:T(8,128)}, /*index=5...) custom-call(s32[2]{0:T(128)} %lengths.3, f32[2,256,768]{2,1,0:T(8,128)} %inputs.3, ...), custom_call_target="tpu_custom_call" | custom-call | tf_op jit(solution)/shard_map/back/pallas_call | solution.py:1473
  436.6 1.6 slice_reduce_fusion
  438.2 0.0 copy-done.4
  438.2 0.6 fusion.2
  440.1 0.0 copy-start.2
  440.1 5.1 %reverse_select_fusion = (f32[2,256,768]{2,1,0:T(8,128)}, f32[2,256,768]{2,1,0:T(8,128)}) fusion(f32[2,256,768]{2,1,0:T(8,128)} %bitcast.10, pred[]{:T(512)} %bitcast, f32[2,256,768]{2,1,0:T(8,128)} %bitcast.9), kind=kLoop, calls=%fused_computation | loop fusion | flops 786432 | bytes 6291457 | tf_op jit(solution)/shard_map/jit(_where)/select_n | solution.py:1604
  445.2 0.0 copy-done.2
  445.2 0.0 copy-start.1
  445.2 1.4 fusion
  446.6 0.7 fusion.1
  447.3 0.4 copy-done.1
  447.7 0.0 copy-start
  447.7 1.4 copy.42
  449.1 1.1 copy-done
  450.2 1.4 copy.43
Async XLA Ops:
  0.7 7.0 %copy-start.3 = (f32[768,192]{0,1:T(8,128)S(1)}, f32[768,192]{0,1:T(8,128)}, u32[]{:S(2)}) copy-start(f32[768,192]{0,1:T(8,128)} %param.25) | copy-start | bytes 1769476
  8.8 34.4 %copy-start.5 = (f32[768]{0:T(1024)S(1)}, f32[768]{0:T(1024)}, u32[]{:S(2)}) copy-start(f32[768]{0:T(1024)} %param.30) | copy-start | bytes 9220
  8.8 35.0 %copy-start.6 = (f32[768]{0:T(1024)S(1)}, f32[768]{0:T(1024)}, u32[]{:S(2)}) copy-start(f32[768]{0:T(1024)} %param.31) | copy-start | bytes 9220
  8.8 35.6 %copy-start.7 = (f32[768]{0:T(1024)S(1)}, f32[768]{0:T(1024)}, u32[]{:S(2)}) copy-start(f32[768]{0:T(1024)} %param.32) | copy-start | bytes 9220
  8.8 36.1 %copy-start.8 = (f32[768]{0:T(1024)S(1)}, f32[768]{0:T(1024)}, u32[]{:S(2)}) copy-start(f32[768]{0:T(1024)} %param.34) | copy-start | bytes 9220
  8.8 36.7 %copy-start.9 = (f32[768]{0:T(1024)S(1)}, f32[768]{0:T(1024)}, u32[]{:S(2)}) copy-start(f32[768]{0:T(1024)} %param.36) | copy-start | bytes 9220
  46.2 392.0 %copy-start.4 = (s32[2]{0:T(128)S(1)}, s32[2]{0:T(128)}, u32[]{:S(2)}) copy-start(s32[2]{0:T(128)} %lengths.3) | copy-start | bytes 28
  440.1 5.1 %copy-start.2 = (f32[784,768]{1,0:T(8,128)S(1)}, f32[784,768]{1,0:T(8,128)}, u32[]{:S(2)}) copy-start(f32[784,768]{1,0:T(8,128)} %get-tuple-element.43) | copy-start | bytes 7225348
  445.2 2.5 copy-start.1
  447.7 2.5 copy-start
